TPU v7x, 512 devices: a whole 4x8x8 slice. The times are simulated.
512 devices in a mesh: ta: 128 (over y_hi, x, z), gz: 4 (over y_lo, core).
Axes of the slice: x: 4, y: 8 (y_hi: 4, y_lo: 2; y = y_hi * 2 + y_lo), z: 8, core: 2. Of those that a mesh axis runs over, the one named last changes fastest.
Arguments:
- source: bfloat16 [128, 8, 4, 4, 64, 128], P('ta', 'gz'), may hold values from -6 to 6
- self_codes: bfloat16 [128, 8, 4, 4, 64, 64], P('ta', 'gz'), may hold values from -6 to 6
- hop_codes: bfloat16 [128, 8, 4, 4, 64, 256], P('ta', 'gz'), may hold values from -6 to 6
- link_scales: bfloat16 [128, 8, 4, 4, 5], P('ta', 'gz'), may hold values from 0.019897461 to 0.079589844
- restrict_map: int32 [128, 8, 4, 4], P('ta', 'gz'), may hold values from 0 to 15
- restrictor: bfloat16 [128, 8, 4, 4, 64, 64], P('ta', 'gz'), may hold values from -0.75 to 0.75
Outputs:
- smoothed: bfloat16 [128, 8, 4, 4, 64, 128], P('ta', 'gz')
- coarse: float32 [128, 16, 64, 128], P('ta', 'gz')
All inputs are finite; a program needn't handle non-finite values.
Results may differ from a plain program's by a relative error of at most 0.0041.
Values may be sent and summed in bfloat16 or wider, within the bound.
No kernel may reach another device: no remote copies, remote signals or barrier semaphores. Data moves between devices by JAX's collectives and lax.ppermute only.
A program may use at most 64 MiB of HBM per device.

v0:
```python
import jax
import jax.numpy as jnp
from jax import lax
from jax.sharding import PartitionSpec as P

ITERS = 3
AGG_DEV = 4
OMEGA = 0.5


def shifted(block, axis, distance):
    devices = range(lax.axis_size(axis))
    route = [((i - distance) % len(devices), i) for i in devices]
    return lax.ppermute(block, axis, route)


def local_mult(codes, vector):
    return jnp.einsum("tzxyab,tzxybr->tzxyar", codes, vector, preferred_element_type=jnp.float32)


def local_mult_transposed(codes, vector):
    return jnp.einsum("tzxyab,tzxyar->tzxybr", codes, vector, preferred_element_type=jnp.float32)


def shards(source, self_codes, hop_codes, link_scales, restrict_map, restrictor):
    degrees = source.shape[4]
    blocks = [
        hop_codes[..., direction * degrees : (direction + 1) * degrees] for direction in range(4)
    ]
    scales = link_scales.astype(jnp.float32)
    factors = [scales[..., direction][..., None, None] for direction in range(5)]
    source_float = source.astype(jnp.float32)
    estimate = source_float
    vector_field = source
    for iteration in range(ITERS):
        result = vector_field.astype(jnp.float32) + factors[0] * local_mult(
            self_codes, vector_field
        )
        arrived = shifted(vector_field, "ta", -1)
        t_next = jnp.concatenate([vector_field[1:], arrived], axis=0)
        z_arrived = shifted(vector_field[:, :1], "gz", -1)
        z_next = jnp.concatenate([vector_field[:, 1:], z_arrived], axis=1)
        neighbours = [jnp.roll(vector_field, -1, 2), jnp.roll(vector_field, -1, 3), z_next, t_next]
        for operate_direction in range(4):
            result = result + factors[operate_direction + 1] * local_mult(
                blocks[operate_direction], neighbours[operate_direction]
            )
        for operate_direction in range(2):
            behind_term = (
                factors[operate_direction + 1]
                * local_mult_transposed(blocks[operate_direction], vector_field)
            ).astype(jnp.bfloat16)
            result = result + jnp.roll(behind_term, 1, axis=2 + operate_direction).astype(
                jnp.float32
            )
        z_terms = (factors[3] * local_mult_transposed(blocks[2], vector_field)).astype(jnp.bfloat16)
        z_from = shifted(z_terms[:, -1:], "gz", 1)
        result = result + jnp.concatenate([z_from, z_terms[:, :-1]], axis=1).astype(jnp.float32)
        t_terms = (factors[4] * local_mult_transposed(blocks[3], vector_field)).astype(jnp.bfloat16)
        t_from = shifted(t_terms, "ta", 1)
        t_incoming = jnp.concatenate([t_from, t_terms[:-1]], axis=0)
        applied = result + t_incoming.astype(jnp.float32)
        estimate = estimate + OMEGA * (source_float - applied)
        vector_field = estimate.astype(jnp.bfloat16)
    coarse_width = restrictor.shape[4]
    right_cols = source.shape[5]
    site_count = source.shape[0] * source.shape[1] * source.shape[2] * source.shape[3]
    projected = jnp.einsum(
        "tzxyca,tzxyar->tzxycr", restrictor, vector_field, preferred_element_type=jnp.float32
    )
    flattened = projected.reshape(site_count, coarse_width * right_cols)
    groups = AGG_DEV * lax.axis_size("gz")
    labels = restrict_map.reshape(site_count)
    onehot = (labels[None, :] == jnp.arange(groups, dtype=jnp.int32)[:, None]).astype(jnp.float32)
    partial_sums = jnp.dot(onehot, flattened, precision=lax.Precision.HIGHEST)
    summed = lax.psum(partial_sums, "gz")
    owned = lax.dynamic_slice_in_dim(summed, lax.axis_index("gz") * AGG_DEV, AGG_DEV, 0)
    return (vector_field, owned.reshape(1, AGG_DEV, coarse_width, right_cols))


def solution(mesh):
    placed = (
        P("ta", "gz", None, None, None, None),
        P("ta", "gz", None, None, None, None),
        P("ta", "gz", None, None, None, None),
        P("ta", "gz", None, None, None),
        P("ta", "gz", None, None),
        P("ta", "gz", None, None, None, None),
    )
    return jax.shard_map(
        shards,
        mesh=mesh,
        in_specs=placed,
        out_specs=(P("ta", "gz", None, None, None, None), P("ta", "gz", None, None)),
        check_vma=False,
    )
```

profile of v0, /device:TPU:1, one launch (start us, length us, event | category | flops | bytes accessed | tf_op | source)
XLA Modules:
  0.0 201.6 jit_solution(1051310907819398375)
XLA Ops:
  7.2 17.5 %collective-permute-start.1 = (bf16[1,2,4,4,64,128]{5,4,3,2,1,0:T(8,128)(2,1)}, bf16[1,2,4,4,64,128]{5,4,3,2,1,0:T(8,128)(2,1)}, u32[]{:S(2)}, u32[]{:S(2)}) collective-permute-start(bf16[1,2,4,4,64,128]{5,4,3,2,1,0:T(8,128)(2,1)} %param.6), channel_id=1, source_target_pairs={{4,0},{8,4},{12,8},{16,12},{20,16},{24,20},{28,24},{32,28},{36,32}... | collective-permute-start | bytes 1572872 | tf_op jit(solution)/shard_map/ppermute | solution.py:14
  24.8 0.7 convert_element_type.228
  25.7 1.6 fusion.66
  27.4 0.8 fusion.176
  28.1 3.1 %collective-permute-start.2 = (bf16[1,1,4,4,64,128]{5,4,3,2,1,0:T(8,128)(2,1)}, bf16[1,1,4,4,64,128]{5,4,3,2,1,0:T(8,128)(2,1)}, u32[]{:S(2)}, u32[]{:S(2)}) collective-permute-start(bf16[1,1,4,4,64,128]{5,4,3,2,1,0:T(8,128)(2,1)} %get-tuple-element.15), channel_id=1, source_target_pairs={{3,0},{0,1},{1,2},{2,3},{7,4},{4,5},{5,6},{6,7},{11,8},{8,9},{9,10... | collective-permute-start | bytes 786440 | tf_op jit(solution)/shard_map/ppermute | solution.py:14
  31.3 1.4 fusion.65
  32.7 1.9 collective-permute-start.3
  34.6 0.9 fusion.177
  35.5 1.9 collective-permute-start
  38.5 0.7 copy-done.4
  39.6 0.6 fusion.67
  40.2 0.8 copy-done.6
  41.0 0.7 copy-done.12
  41.8 5.1 %collective-permute-done.1 = bf16[1,2,4,4,64,128]{5,4,3,2,1,0:T(8,128)(2,1)} collective-permute-done((bf16[1,2,4,4,64,128]{5,4,3,2,1,0:T(8,128)(2,1)}, bf16[1,2,4,4,64,128]{5,4,3,2,1,0:T(8,128)(2,1)}, u32[]{:S(2)}, u32[]{:S(2)}) %collective-permute-start.1) | collective-permute-done | bytes 524320 | tf_op jit(solution)/shard_map/ppermute | solution.py:14
  46.9 1.4 fusion.13
  48.3 5.4 %collective-permute-done = bf16[1,1,4,4,64,128]{5,4,3,2,1,0:T(8,128)(2,1)} collective-permute-done((bf16[1,1,4,4,64,128]{5,4,3,2,1,0:T(8,128)(2,1)}, bf16[1,1,4,4,64,128]{5,4,3,2,1,0:T(8,128)(2,1)}, u32[]{:S(2)}, u32[]{:S(2)}) %collective-permute-start) | collective-permute-done | bytes 262176 | tf_op jit(solution)/shard_map/ppermute | solution.py:14
  53.7 12.5 %collective-permute-done.3 = bf16[1,2,4,4,64,128]{5,4,3,2,1,0:T(8,128)(2,1)} collective-permute-done((bf16[1,2,4,4,64,128]{5,4,3,2,1,0:T(8,128)(2,1)}, bf16[1,2,4,4,64,128]{5,4,3,2,1,0:T(8,128)(2,1)}, u32[]{:S(2)}, u32[]{:S(2)}) %collective-permute-start.3) | collective-permute-done | bytes 524320 | tf_op jit(solution)/shard_map/ppermute | solution.py:14
  66.2 1.9 fusion.178
  68.2 1.9 collective-permute-start.5
  70.5 0.6 fusion.61
  71.5 0.8 copy-done.7
  72.4 2.1 %collective-permute-start.6 = (bf16[1,1,4,4,64,128]{5,4,3,2,1,0:T(8,128)(2,1)S(1)}, bf16[1,1,4,4,64,128]{5,4,3,2,1,0:T(8,128)(2,1)S(1)}, u32[]{:S(2)}, u32[]{:S(2)}) collective-permute-start(bf16[1,1,4,4,64,128]{5,4,3,2,1,0:T(8,128)(2,1)S(1)} %get-tuple-element.11), channel_id=1, source_target_pairs={{3,0},{0,1},{1,2},{2,3},{7,4},{4,5},{5,6},{6,7},{11,8},{8,9},{9,10... | collective-permute-start | bytes 786440 | tf_op jit(solution)/shard_map/ppermute | solution.py:14
  74.5 3.6 %collective-permute-start.7 = (bf16[1,2,4,4,64,128]{5,4,3,2,1,0:T(8,128)(2,1)S(1)}, bf16[1,2,4,4,64,128]{5,4,3,2,1,0:T(8,128)(2,1)S(1)}, u32[]{:S(2)}, u32[]{:S(2)}) collective-permute-start(bf16[1,2,4,4,64,128]{5,4,3,2,1,0:T(8,128)(2,1)S(1)} %fusion.61), channel_id=1, source_target_pairs={{508,0},{0,4},{4,8},{8,12},{12,16},{16,20},{20,24},{24,28},{28,32}... | collective-permute-start | bytes 1572872 | tf_op jit(solution)/shard_map/ppermute | solution.py:14
  78.1 2.8 %collective-permute-start.4 = (bf16[1,1,4,4,64,128]{5,4,3,2,1,0:T(8,128)(2,1)S(1)}, bf16[1,1,4,4,64,128]{5,4,3,2,1,0:T(8,128)(2,1)S(1)}, u32[]{:S(2)}, u32[]{:S(2)}) collective-permute-start(bf16[1,1,4,4,64,128]{5,4,3,2,1,0:T(8,128)(2,1)S(1)} %get-tuple-element.14), channel_id=1, source_target_pairs={{1,0},{2,1},{3,2},{0,3},{5,4},{6,5},{7,6},{4,7},{9,8},{10,9},{11,1... | collective-permute-start | bytes 786440 | tf_op jit(solution)/shard_map/ppermute | solution.py:14
  82.0 0.6 fusion.63
  82.7 0.8 copy-done.8
  83.5 9.1 %collective-permute-done.5 = bf16[1,2,4,4,64,128]{5,4,3,2,1,0:T(8,128)(2,1)S(1)} collective-permute-done((bf16[1,2,4,4,64,128]{5,4,3,2,1,0:T(8,128)(2,1)S(1)}, bf16[1,2,4,4,64,128]{5,4,3,2,1,0:T(8,128)(2,1)S(1)}, u32[]{:S(2)}, u32[]{:S(2)}) %collective-permute-start.5) | collective-permute-done | bytes 524320 | tf_op jit(solution)/shard_map/ppermute | solution.py:14
  93.0 10.9 %collective-permute-done.7 = bf16[1,2,4,4,64,128]{5,4,3,2,1,0:T(8,128)(2,1)S(1)} collective-permute-done((bf16[1,2,4,4,64,128]{5,4,3,2,1,0:T(8,128)(2,1)S(1)}, bf16[1,2,4,4,64,128]{5,4,3,2,1,0:T(8,128)(2,1)S(1)}, u32[]{:S(2)}, u32[]{:S(2)}) %collective-permute-start.7) | collective-permute-done | bytes 524320 | tf_op jit(solution)/shard_map/ppermute | solution.py:14
  103.9 0.7 fusion.179
  104.7 1.9 collective-permute-start.9
  106.7 0.4 fusion.58
  107.0 0.6 fusion.57
  107.7 0.4 fusion.60
  108.1 0.7 copy-done.3
  108.9 7.5 %collective-permute-start.10 = (bf16[1,1,4,4,64,128]{5,4,3,2,1,0:T(8,128)(2,1)S(1)}, bf16[1,1,4,4,64,128]{5,4,3,2,1,0:T(8,128)(2,1)S(1)}, u32[]{:S(2)}, u32[]{:S(2)}) collective-permute-start(bf16[1,1,4,4,64,128]{5,4,3,2,1,0:T(8,128)(2,1)S(1)} %get-tuple-element.7), channel_id=1, source_target_pairs={{3,0},{0,1},{1,2},{2,3},{7,4},{4,5},{5,6},{6,7},{11,8},{8,9},{9,10... | collective-permute-start | bytes 786440 | tf_op jit(solution)/shard_map/ppermute | solution.py:14
  116.4 3.6 %collective-permute-start.11 = (bf16[1,2,4,4,64,128]{5,4,3,2,1,0:T(8,128)(2,1)S(1)}, bf16[1,2,4,4,64,128]{5,4,3,2,1,0:T(8,128)(2,1)S(1)}, u32[]{:S(2)}, u32[]{:S(2)}) collective-permute-start(bf16[1,2,4,4,64,128]{5,4,3,2,1,0:T(8,128)(2,1)S(1)} %fusion.57), channel_id=1, source_target_pairs={{508,0},{0,4},{4,8},{8,12},{12,16},{16,20},{20,24},{24,28},{28,32}... | collective-permute-start | bytes 1572872 | tf_op jit(solution)/shard_map/ppermute | solution.py:14
  120.0 2.1 %collective-permute-start.8 = (bf16[1,1,4,4,64,128]{5,4,3,2,1,0:T(8,128)(2,1)S(1)}, bf16[1,1,4,4,64,128]{5,4,3,2,1,0:T(8,128)(2,1)S(1)}, u32[]{:S(2)}, u32[]{:S(2)}) collective-permute-start(bf16[1,1,4,4,64,128]{5,4,3,2,1,0:T(8,128)(2,1)S(1)} %get-tuple-element.10), channel_id=1, source_target_pairs={{1,0},{2,1},{3,2},{0,3},{5,4},{6,5},{7,6},{4,7},{9,8},{10,9},{11,1... | collective-permute-start | bytes 786440 | tf_op jit(solution)/shard_map/ppermute | solution.py:14
  122.8 0.4 fusion.35
  123.2 0.6 fusion.59
  123.9 0.8 copy-done.5
  125.0 11.4 %collective-permute-done.8 = bf16[1,1,4,4,64,128]{5,4,3,2,1,0:T(8,128)(2,1)S(1)} collective-permute-done((bf16[1,1,4,4,64,128]{5,4,3,2,1,0:T(8,128)(2,1)S(1)}, bf16[1,1,4,4,64,128]{5,4,3,2,1,0:T(8,128)(2,1)S(1)}, u32[]{:S(2)}, u32[]{:S(2)}) %collective-permute-start.8) | collective-permute-done | bytes 262176 | tf_op jit(solution)/shard_map/ppermute | solution.py:14
  136.5 11.5 %collective-permute-done.11 = bf16[1,2,4,4,64,128]{5,4,3,2,1,0:T(8,128)(2,1)S(1)} collective-permute-done((bf16[1,2,4,4,64,128]{5,4,3,2,1,0:T(8,128)(2,1)S(1)}, bf16[1,2,4,4,64,128]{5,4,3,2,1,0:T(8,128)(2,1)S(1)}, u32[]{:S(2)}, u32[]{:S(2)}) %collective-permute-start.11) | collective-permute-done | bytes 524320 | tf_op jit(solution)/shard_map/ppermute | solution.py:14
  148.1 0.7 fusion.44
  149.4 0.5 copy-done.9
  149.9 1.9 fusion.69
  151.8 41.3 %all-reduce.2.cloned.1.call-done = f32[16,8192]{1,0:T(8,128)} async-done(((f32[16,8192]{1,0:T(8,128)}), f32[16,8192]{1,0:T(8,128)}) %all-reduce.2.cloned.1.call-update) | async-done | bytes 524304 | tf_op jit(solution)/shard_map/psum | solution.py:76
  193.2 1.0 dynamic-slice_bitcast_fusion
  194.1 0.7 copy.51
  (81 shorter events, 5.8 us)
Async XLA Ops:
  7.2 30.3 %copy-start = (bf16[1,2,4,4,64,64]{5,4,3,2,1,0:T(8,128)(2,1)S(1)}, bf16[1,2,4,4,64,64]{5,4,3,2,1,0:T(8,128)(2,1)}, u32[]{:S(2)}) copy-start(bf16[1,2,4,4,64,64]{5,4,3,2,1,0:T(8,128)(2,1)} %param.7) | copy-start | bytes 786436
  7.2 186.0 %all-reduce.2.cloned.1.call-start = ((), (), s32[]{:S(2)}) async-start(), calls=%async_computation | async-start | bytes 1048576 | tf_op jit(solution)/shard_map/psum | solution.py:76
  7.2 39.7 %collective-permute-start.1 = (bf16[1,2,4,4,64,128]{5,4,3,2,1,0:T(8,128)(2,1)}, bf16[1,2,4,4,64,128]{5,4,3,2,1,0:T(8,128)(2,1)}, u32[]{:S(2)}, u32[]{:S(2)}) collective-permute-start(bf16[1,2,4,4,64,128]{5,4,3,2,1,0:T(8,128)(2,1)} %param.6), channel_id=1, source_target_pairs={{4,0},{8,4},{12,8},{16,12},{20,16},{24,20},{28,24},{32,28},{36,32}... | collective-permute-start | bytes 1572872 | tf_op jit(solution)/shard_map/ppermute | solution.py:14
  25.7 5.6 %copy-start.1 = (bf16[1,2,4,4,64,256]{5,4,3,2,1,0:T(8,128)(2,1)S(1)}, bf16[1,2,4,4,64,256]{5,4,3,2,1,0:T(8,128)(2,1)}, u32[]{:S(2)}) copy-start(bf16[1,2,4,4,64,256]{5,4,3,2,1,0:T(8,128)(2,1)} %param.8) | copy-start | bytes 3145732
  27.3 3.9 %copy-start.2 = (bf16[1,2,4,4,64,128]{5,4,3,2,1,0:T(8,128)(2,1)S(1)}, bf16[1,2,4,4,64,128]{5,4,3,2,1,0:T(8,128)(2,1)}, u32[]{:S(2)}) copy-start(bf16[1,2,4,4,64,128]{5,4,3,2,1,0:T(8,128)(2,1)} %param.6) | copy-start | bytes 1572868
  28.1 20.2 %collective-permute-start.2 = (bf16[1,1,4,4,64,128]{5,4,3,2,1,0:T(8,128)(2,1)}, bf16[1,1,4,4,64,128]{5,4,3,2,1,0:T(8,128)(2,1)}, u32[]{:S(2)}, u32[]{:S(2)}) collective-permute-start(bf16[1,1,4,4,64,128]{5,4,3,2,1,0:T(8,128)(2,1)} %get-tuple-element.15), channel_id=1, source_target_pairs={{3,0},{0,1},{1,2},{2,3},{7,4},{4,5},{5,6},{6,7},{11,8},{8,9},{9,10... | collective-permute-start | bytes 786440 | tf_op jit(solution)/shard_map/ppermute | solution.py:14
  32.7 33.5 %collective-permute-start.3 = (bf16[1,2,4,4,64,128]{5,4,3,2,1,0:T(8,128)(2,1)}, bf16[1,2,4,4,64,128]{5,4,3,2,1,0:T(8,128)(2,1)}, u32[]{:S(2)}, u32[]{:S(2)}) collective-permute-start(bf16[1,2,4,4,64,128]{5,4,3,2,1,0:T(8,128)(2,1)} %fusion.65), channel_id=1, source_target_pairs={{508,0},{0,4},{4,8},{8,12},{12,16},{16,20},{20,24},{24,28},{28,32}... | collective-permute-start | bytes 1572872 | tf_op jit(solution)/shard_map/ppermute | solution.py:14
  35.5 18.3 %collective-permute-start = (bf16[1,1,4,4,64,128]{5,4,3,2,1,0:T(8,128)(2,1)}, bf16[1,1,4,4,64,128]{5,4,3,2,1,0:T(8,128)(2,1)}, u32[]{:S(2)}, u32[]{:S(2)}) collective-permute-start(bf16[1,1,4,4,64,128]{5,4,3,2,1,0:T(8,128)(2,1)} %get-tuple-element.18), channel_id=1, source_target_pairs={{1,0},{2,1},{3,2},{0,3},{5,4},{6,5},{7,6},{4,7},{9,8},{10,9},{11,1... | collective-permute-start | bytes 786440 | tf_op jit(solution)/shard_map/ppermute | solution.py:14
  38.5 0.8 copy-start.4
  40.2 0.8 copy-start.6
  41.0 0.7 copy-start.12
  41.8 24.4 %slice-start.2 = ((bf16[1,2,4,4,64,128]{5,4,3,2,1,0:T(8,128)(2,1)}), bf16[1,2,3,4,64,128]{5,4,3,2,1,0:T(8,128)(2,1)S(1)}, s32[]{:S(2)}) async-start(bf16[1,2,4,4,64,128]{5,4,3,2,1,0:T(8,128)(2,1)} %copy-done.4), calls=%async_computation.3 | async-start | bytes 786432 | tf_op jit(solution)/shard_map/jit(_roll_static)/slice | solution.py:53
  41.8 24.4 %slice-start.3 = ((bf16[1,2,4,4,64,128]{5,4,3,2,1,0:T(8,128)(2,1)}), bf16[1,2,1,4,64,128]{5,4,3,2,1,0:T(8,128)(2,1)S(1)}, s32[]{:S(2)}) async-start(bf16[1,2,4,4,64,128]{5,4,3,2,1,0:T(8,128)(2,1)} %copy-done.4), calls=%async_computation.4 | async-start | bytes 262144 | tf_op jit(solution)/shard_map/jit(_roll_static)/slice | solution.py:53
  41.8 24.4 %slice-start.6 = ((bf16[1,2,4,4,64,128]{5,4,3,2,1,0:T(8,128)(2,1)}), bf16[1,2,4,3,64,128]{5,4,3,2,1,0:T(8,128)(2,1)S(1)}, s32[]{:S(2)}) async-start(bf16[1,2,4,4,64,128]{5,4,3,2,1,0:T(8,128)(2,1)} %copy-done.6), calls=%async_computation.7 | async-start | bytes 786432 | tf_op jit(solution)/shard_map/jit(_roll_static)/slice | solution.py:53
  41.8 24.4 %slice-start.7 = ((bf16[1,2,4,4,64,128]{5,4,3,2,1,0:T(8,128)(2,1)}), bf16[1,2,4,1,64,128]{5,4,3,2,1,0:T(8,128)(2,1)S(1)}, s32[]{:S(2)}) async-start(bf16[1,2,4,4,64,128]{5,4,3,2,1,0:T(8,128)(2,1)} %copy-done.6), calls=%async_computation.8 | async-start | bytes 262144 | tf_op jit(solution)/shard_map/jit(_roll_static)/slice | solution.py:53
  41.8 24.4 %copy-start.10 = (bf16[1,1,4,4,64,128]{5,4,3,2,1,0:T(8,128)(2,1)S(1)}, bf16[1,1,4,4,64,128]{5,4,3,2,1,0:T(8,128)(2,1)}, u32[]{:S(2)}) copy-start(bf16[1,1,4,4,64,128]{5,4,3,2,1,0:T(8,128)(2,1)} %get-tuple-element.17) | copy-start | bytes 786436
  68.2 24.4 %collective-permute-start.5 = (bf16[1,2,4,4,64,128]{5,4,3,2,1,0:T(8,128)(2,1)S(1)}, bf16[1,2,4,4,64,128]{5,4,3,2,1,0:T(8,128)(2,1)S(1)}, u32[]{:S(2)}, u32[]{:S(2)}) collective-permute-start(bf16[1,2,4,4,64,128]{5,4,3,2,1,0:T(8,128)(2,1)S(1)} %get-tuple-element.19), channel_id=1, source_target_pairs={{4,0},{8,4},{12,8},{16,12},{20,16},{24,20},{28,24},{32,28},{36,32}... | collective-permute-start | bytes 1572872 | tf_op jit(solution)/shard_map/ppermute | solution.py:14
  71.5 0.8 copy-start.7
  72.4 20.5 %collective-permute-start.6 = (bf16[1,1,4,4,64,128]{5,4,3,2,1,0:T(8,128)(2,1)S(1)}, bf16[1,1,4,4,64,128]{5,4,3,2,1,0:T(8,128)(2,1)S(1)}, u32[]{:S(2)}, u32[]{:S(2)}) collective-permute-start(bf16[1,1,4,4,64,128]{5,4,3,2,1,0:T(8,128)(2,1)S(1)} %get-tuple-element.11), channel_id=1, source_target_pairs={{3,0},{0,1},{1,2},{2,3},{7,4},{4,5},{5,6},{6,7},{11,8},{8,9},{9,10... | collective-permute-start | bytes 786440 | tf_op jit(solution)/shard_map/ppermute | solution.py:14
  74.5 29.4 %collective-permute-start.7 = (bf16[1,2,4,4,64,128]{5,4,3,2,1,0:T(8,128)(2,1)S(1)}, bf16[1,2,4,4,64,128]{5,4,3,2,1,0:T(8,128)(2,1)S(1)}, u32[]{:S(2)}, u32[]{:S(2)}) collective-permute-start(bf16[1,2,4,4,64,128]{5,4,3,2,1,0:T(8,128)(2,1)S(1)} %fusion.61), channel_id=1, source_target_pairs={{508,0},{0,4},{4,8},{8,12},{12,16},{16,20},{20,24},{24,28},{28,32}... | collective-permute-start | bytes 1572872 | tf_op jit(solution)/shard_map/ppermute | solution.py:14
  78.1 14.8 %collective-permute-start.4 = (bf16[1,1,4,4,64,128]{5,4,3,2,1,0:T(8,128)(2,1)S(1)}, bf16[1,1,4,4,64,128]{5,4,3,2,1,0:T(8,128)(2,1)S(1)}, u32[]{:S(2)}, u32[]{:S(2)}) collective-permute-start(bf16[1,1,4,4,64,128]{5,4,3,2,1,0:T(8,128)(2,1)S(1)} %get-tuple-element.14), channel_id=1, source_target_pairs={{1,0},{2,1},{3,2},{0,3},{5,4},{6,5},{7,6},{4,7},{9,8},{10,9},{11,1... | collective-permute-start | bytes 786440 | tf_op jit(solution)/shard_map/ppermute | solution.py:14
  82.6 0.8 copy-start.8
  83.4 20.5 %slice-start.8 = ((bf16[1,2,4,4,64,128]{5,4,3,2,1,0:T(8,128)(2,1)}), bf16[1,2,3,4,64,128]{5,4,3,2,1,0:T(8,128)(2,1)S(1)}, s32[]{:S(2)}) async-start(bf16[1,2,4,4,64,128]{5,4,3,2,1,0:T(8,128)(2,1)} %copy-done.7), calls=%async_computation.9 | async-start | bytes 786432 | tf_op jit(solution)/shard_map/jit(_roll_static)/slice | solution.py:53
  83.4 20.5 %slice-start.9 = ((bf16[1,2,4,4,64,128]{5,4,3,2,1,0:T(8,128)(2,1)}), bf16[1,2,1,4,64,128]{5,4,3,2,1,0:T(8,128)(2,1)S(1)}, s32[]{:S(2)}) async-start(bf16[1,2,4,4,64,128]{5,4,3,2,1,0:T(8,128)(2,1)} %copy-done.7), calls=%async_computation.10 | async-start | bytes 262144 | tf_op jit(solution)/shard_map/jit(_roll_static)/slice | solution.py:53
  83.4 20.5 %slice-start.10 = ((bf16[1,2,4,4,64,128]{5,4,3,2,1,0:T(8,128)(2,1)}), bf16[1,2,4,3,64,128]{5,4,3,2,1,0:T(8,128)(2,1)S(1)}, s32[]{:S(2)}) async-start(bf16[1,2,4,4,64,128]{5,4,3,2,1,0:T(8,128)(2,1)} %copy-done.8), calls=%async_computation.11 | async-start | bytes 786432 | tf_op jit(solution)/shard_map/jit(_roll_static)/slice | solution.py:53
  83.5 20.5 %slice-start.11 = ((bf16[1,2,4,4,64,128]{5,4,3,2,1,0:T(8,128)(2,1)}), bf16[1,2,4,1,64,128]{5,4,3,2,1,0:T(8,128)(2,1)S(1)}, s32[]{:S(2)}) async-start(bf16[1,2,4,4,64,128]{5,4,3,2,1,0:T(8,128)(2,1)} %copy-done.8), calls=%async_computation.12 | async-start | bytes 262144 | tf_op jit(solution)/shard_map/jit(_roll_static)/slice | solution.py:53
  104.7 19.9 %collective-permute-start.9 = (bf16[1,2,4,4,64,128]{5,4,3,2,1,0:T(8,128)(2,1)S(1)}, bf16[1,2,4,4,64,128]{5,4,3,2,1,0:T(8,128)(2,1)S(1)}, u32[]{:S(2)}, u32[]{:S(2)}) collective-permute-start(bf16[1,2,4,4,64,128]{5,4,3,2,1,0:T(8,128)(2,1)S(1)} %get-tuple-element.21), channel_id=1, source_target_pairs={{4,0},{8,4},{12,8},{16,12},{20,16},{24,20},{28,24},{32,28},{36,32}... | collective-permute-start | bytes 1572872 | tf_op jit(solution)/shard_map/ppermute | solution.py:14
  108.0 0.8 copy-start.3
  108.9 16.2 %collective-permute-start.10 = (bf16[1,1,4,4,64,128]{5,4,3,2,1,0:T(8,128)(2,1)S(1)}, bf16[1,1,4,4,64,128]{5,4,3,2,1,0:T(8,128)(2,1)S(1)}, u32[]{:S(2)}, u32[]{:S(2)}) collective-permute-start(bf16[1,1,4,4,64,128]{5,4,3,2,1,0:T(8,128)(2,1)S(1)} %get-tuple-element.7), channel_id=1, source_target_pairs={{3,0},{0,1},{1,2},{2,3},{7,4},{4,5},{5,6},{6,7},{11,8},{8,9},{9,10... | collective-permute-start | bytes 786440 | tf_op jit(solution)/shard_map/ppermute | solution.py:14
  116.4 31.7 %collective-permute-start.11 = (bf16[1,2,4,4,64,128]{5,4,3,2,1,0:T(8,128)(2,1)S(1)}, bf16[1,2,4,4,64,128]{5,4,3,2,1,0:T(8,128)(2,1)S(1)}, u32[]{:S(2)}, u32[]{:S(2)}) collective-permute-start(bf16[1,2,4,4,64,128]{5,4,3,2,1,0:T(8,128)(2,1)S(1)} %fusion.57), channel_id=1, source_target_pairs={{508,0},{0,4},{4,8},{8,12},{12,16},{16,20},{20,24},{24,28},{28,32}... | collective-permute-start | bytes 1572872 | tf_op jit(solution)/shard_map/ppermute | solution.py:14
  120.0 16.5 %collective-permute-start.8 = (bf16[1,1,4,4,64,128]{5,4,3,2,1,0:T(8,128)(2,1)S(1)}, bf16[1,1,4,4,64,128]{5,4,3,2,1,0:T(8,128)(2,1)S(1)}, u32[]{:S(2)}, u32[]{:S(2)}) collective-permute-start(bf16[1,1,4,4,64,128]{5,4,3,2,1,0:T(8,128)(2,1)S(1)} %get-tuple-element.10), channel_id=1, source_target_pairs={{1,0},{2,1},{3,2},{0,3},{5,4},{6,5},{7,6},{4,7},{9,8},{10,9},{11,1... | collective-permute-start | bytes 786440 | tf_op jit(solution)/shard_map/ppermute | solution.py:14
  123.9 0.8 copy-start.5
  124.6 23.4 %slice-start = ((bf16[1,2,4,4,64,128]{5,4,3,2,1,0:T(8,128)(2,1)}), bf16[1,2,3,4,64,128]{5,4,3,2,1,0:T(8,128)(2,1)S(1)}, s32[]{:S(2)}) async-start(bf16[1,2,4,4,64,128]{5,4,3,2,1,0:T(8,128)(2,1)} %copy-done.3), calls=%async_computation.1 | async-start | bytes 786432 | tf_op jit(solution)/shard_map/jit(_roll_static)/slice | solution.py:53
  124.6 23.4 %slice-start.1 = ((bf16[1,2,4,4,64,128]{5,4,3,2,1,0:T(8,128)(2,1)}), bf16[1,2,1,4,64,128]{5,4,3,2,1,0:T(8,128)(2,1)S(1)}, s32[]{:S(2)}) async-start(bf16[1,2,4,4,64,128]{5,4,3,2,1,0:T(8,128)(2,1)} %copy-done.3), calls=%async_computation.2 | async-start | bytes 262144 | tf_op jit(solution)/shard_map/jit(_roll_static)/slice | solution.py:53
  124.6 23.4 %slice-start.4 = ((bf16[1,2,4,4,64,128]{5,4,3,2,1,0:T(8,128)(2,1)}), bf16[1,2,4,3,64,128]{5,4,3,2,1,0:T(8,128)(2,1)S(1)}, s32[]{:S(2)}) async-start(bf16[1,2,4,4,64,128]{5,4,3,2,1,0:T(8,128)(2,1)} %copy-done.5), calls=%async_computation.5 | async-start | bytes 786432 | tf_op jit(solution)/shard_map/jit(_roll_static)/slice | solution.py:53
  124.6 23.4 %slice-start.5 = ((bf16[1,2,4,4,64,128]{5,4,3,2,1,0:T(8,128)(2,1)}), bf16[1,2,4,1,64,128]{5,4,3,2,1,0:T(8,128)(2,1)S(1)}, s32[]{:S(2)}) async-start(bf16[1,2,4,4,64,128]{5,4,3,2,1,0:T(8,128)(2,1)} %copy-done.5), calls=%async_computation.6 | async-start | bytes 262144 | tf_op jit(solution)/shard_map/jit(_roll_static)/slice | solution.py:53
  148.1 1.0 copy-start.11
  149.1 0.8 copy-start.9
Sparse Core Ops, SparseCore 0:
  151.9 41.1 all-reduce.1
where the time goes:
time: 202 us
  waiting for transfers between devices  107 us (53%)
  starting transfers between devices  50.1 us (25%)
  matrix products  18.6 us (9%)
  between operations  14.7 us (7%)
  local copies, waits for them, and re-layouts  10.1 us (5%)
    ppermute x12, waiting for transfers between devices, shifted(): return lax.ppermute(block, axis, route)  66.1 us
    ppermute x12, starting transfers between devices, shifted(): return lax.ppermute(block, axis, route)  50.1 us
    psum x1, waiting for transfers between devices, shards(): summed = lax.psum(partial_sums, 'gz')  41.3 us
    dot_general x15, matrix products, local_mult(): jnp.einsum('tzxyab,tzxybr->tzxyar', codes, vector, preferred_element_type...  8.42 us
    dot_general x12, matrix products, local_mult_transposed(): jnp.einsum('tzxyab,tzxyar->tzxybr', codes, vector, preferred_element_type...  8.03 us
    unnamed x28, local copies, waits for them, and re-layouts  7.74 us
  transfers between devices with their start and end apart: 13, of which 8 were waited for; matrix products, arithmetic and copies ran while one was open for 8% of the time, Pallas kernels for 0%

commit v1 on v0

--- a/solution.py
+++ b/solution.py
@@ -73,7 +73,7 @@
     labels = restrict_map.reshape(site_count)
     onehot = (labels[None, :] == jnp.arange(groups, dtype=jnp.int32)[:, None]).astype(jnp.float32)
     partial_sums = jnp.dot(onehot, flattened, precision=lax.Precision.HIGHEST)
-    summed = lax.psum(partial_sums, "gz")
+    summed = jnp.sum(lax.all_gather(partial_sums, "gz"), axis=0)
     owned = lax.dynamic_slice_in_dim(summed, lax.axis_index("gz") * AGG_DEV, AGG_DEV, 0)
     return (vector_field, owned.reshape(1, AGG_DEV, coarse_width, right_cols))
 

time: 202 us -> 188 us (0.931)
  waiting for transfers between devices: 107 us -> 94.6 us
  local copies, waits for them, and re-layouts: 10.1 us -> 6.71 us
    psum x1 -> x0, waiting for transfers between devices: 41.3 us -> none  [shards(): summed = lax.psum(partial_sums, 'gz')]
    all_gather x0 -> x1, waiting for transfers between devices: none -> 27.6 us  [shards(): summed = jnp.sum(lax.all_gather(partial_sums, 'gz'), axis=0)]
    unnamed x28 -> x30, local copies, waits for them, and re-layouts: 7.74 us -> 2.93 us
  transfers between devices with their start and end apart: 13 -> 13, of which waited for: 8 -> 8; matrix products, arithmetic and copies ran while one was open for 8% -> 9% of each run, Pallas kernels for 0% -> 0%
where the time goes in v1:
time: 188 us; the launch traced here: 187 us
  waiting for transfers between devices  94.6 us (50%)
  starting transfers between devices  50.1 us (27%)
  matrix products  18.5 us (10%)
  between operations  14.8 us (8%)
  local copies, waits for them, and re-layouts  6.71 us (4%)
  other arithmetic  2.46 us (1%)
    ppermute x12, waiting for transfers between devices, shifted(): return lax.ppermute(block, axis, route)  67 us
    ppermute x12, starting transfers between devices, shifted(): return lax.ppermute(block, axis, route)  50.1 us
    all_gather x1, waiting for transfers between devices, shards(): summed = jnp.sum(lax.all_gather(partial_sums, 'gz'), axis=0)  27.6 us
    dot_general x15, matrix products, local_mult(): jnp.einsum('tzxyab,tzxybr->tzxyar', codes, vector, preferred_element_type...  8.4 us
    dot_general x12, matrix products, local_mult_transposed(): jnp.einsum('tzxyab,tzxyar->tzxybr', codes, vector, preferred_element_type...  7.94 us
  transfers between devices with their start and end apart: 13, of which 8 were waited for; matrix products, arithmetic and copies ran while one was open for 9% of the time, Pallas kernels for 0%

profile of v1, /device:TPU:1, one launch (start us, length us, event | category | flops | bytes accessed | tf_op | source)
XLA Modules:
  0.0 187.1 jit_solution(1455762997884588242)
XLA Ops:
  7.2 17.5 %collective-permute-start.1 = (bf16[1,2,4,4,64,128]{5,4,3,2,1,0:T(8,128)(2,1)}, bf16[1,2,4,4,64,128]{5,4,3,2,1,0:T(8,128)(2,1)}, u32[]{:S(2)}, u32[]{:S(2)}) collective-permute-start(bf16[1,2,4,4,64,128]{5,4,3,2,1,0:T(8,128)(2,1)} %param.6), channel_id=1, source_target_pairs={{4,0},{8,4},{12,8},{16,12},{20,16},{24,20},{28,24},{32,28},{36,32}... | collective-permute-start | bytes 1572872 | tf_op jit(solution)/shard_map/ppermute | solution.py:14
  24.8 0.7 convert_element_type.228
  25.7 1.6 fusion.66
  27.3 0.8 fusion.176
  28.1 3.1 %collective-permute-start.2 = (bf16[1,1,4,4,64,128]{5,4,3,2,1,0:T(8,128)(2,1)}, bf16[1,1,4,4,64,128]{5,4,3,2,1,0:T(8,128)(2,1)}, u32[]{:S(2)}, u32[]{:S(2)}) collective-permute-start(bf16[1,1,4,4,64,128]{5,4,3,2,1,0:T(8,128)(2,1)} %get-tuple-element.15), channel_id=1, source_target_pairs={{3,0},{0,1},{1,2},{2,3},{7,4},{4,5},{5,6},{6,7},{11,8},{8,9},{9,10... | collective-permute-start | bytes 786440 | tf_op jit(solution)/shard_map/ppermute | solution.py:14
  31.3 1.4 fusion.65
  32.7 1.9 %collective-permute-start.3 = (bf16[1,2,4,4,64,128]{5,4,3,2,1,0:T(8,128)(2,1)}, bf16[1,2,4,4,64,128]{5,4,3,2,1,0:T(8,128)(2,1)}, u32[]{:S(2)}, u32[]{:S(2)}) collective-permute-start(bf16[1,2,4,4,64,128]{5,4,3,2,1,0:T(8,128)(2,1)} %fusion.65), channel_id=1, source_target_pairs={{508,0},{0,4},{4,8},{8,12},{12,16},{16,20},{20,24},{24,28},{28,32}... | collective-permute-start | bytes 1572872 | tf_op jit(solution)/shard_map/ppermute | solution.py:14
  34.6 0.8 fusion.177
  35.5 1.9 %collective-permute-start = (bf16[1,1,4,4,64,128]{5,4,3,2,1,0:T(8,128)(2,1)}, bf16[1,1,4,4,64,128]{5,4,3,2,1,0:T(8,128)(2,1)}, u32[]{:S(2)}, u32[]{:S(2)}) collective-permute-start(bf16[1,1,4,4,64,128]{5,4,3,2,1,0:T(8,128)(2,1)} %get-tuple-element.18), channel_id=1, source_target_pairs={{1,0},{2,1},{3,2},{0,3},{5,4},{6,5},{7,6},{4,7},{9,8},{10,9},{11,1... | collective-permute-start | bytes 786440 | tf_op jit(solution)/shard_map/ppermute | solution.py:14
  37.8 0.4 fusion.11
  38.1 0.4 fusion.68
  38.6 0.7 copy-done.4
  39.6 0.6 fusion.67
  40.2 0.8 copy-done.5
  41.0 1.3 eq.15
  42.4 4.5 %collective-permute-done.1 = bf16[1,2,4,4,64,128]{5,4,3,2,1,0:T(8,128)(2,1)} collective-permute-done((bf16[1,2,4,4,64,128]{5,4,3,2,1,0:T(8,128)(2,1)}, bf16[1,2,4,4,64,128]{5,4,3,2,1,0:T(8,128)(2,1)}, u32[]{:S(2)}, u32[]{:S(2)}) %collective-permute-start.1) | collective-permute-done | bytes 524320 | tf_op jit(solution)/shard_map/ppermute | solution.py:14
  46.9 1.4 fusion.13
  48.3 5.4 %collective-permute-done = bf16[1,1,4,4,64,128]{5,4,3,2,1,0:T(8,128)(2,1)} collective-permute-done((bf16[1,1,4,4,64,128]{5,4,3,2,1,0:T(8,128)(2,1)}, bf16[1,1,4,4,64,128]{5,4,3,2,1,0:T(8,128)(2,1)}, u32[]{:S(2)}, u32[]{:S(2)}) %collective-permute-start) | collective-permute-done | bytes 262176 | tf_op jit(solution)/shard_map/ppermute | solution.py:14
  53.8 12.4 %collective-permute-done.3 = bf16[1,2,4,4,64,128]{5,4,3,2,1,0:T(8,128)(2,1)} collective-permute-done((bf16[1,2,4,4,64,128]{5,4,3,2,1,0:T(8,128)(2,1)}, bf16[1,2,4,4,64,128]{5,4,3,2,1,0:T(8,128)(2,1)}, u32[]{:S(2)}, u32[]{:S(2)}) %collective-permute-start.3) | collective-permute-done | bytes 524320 | tf_op jit(solution)/shard_map/ppermute | solution.py:14
  66.3 1.9 %fusion.178 = (bf16[1,2,4,4,64,128]{5,4,3,2,1,0:T(8,128)(2,1)S(1)}, f32[1,2,4,4,64,128]{5,4,3,2,1,0:T(8,128)S(1)}) fusion(bf16[1,2,4,4,64,128]{5,4,3,2,1,0:T(8,128)(2,1)} %collective-permute-done.3, bf16[1,1,4,4,64,128]{5,4,3,2,1,0:T(8,128)(2,1)S(1)} %copy-done.8, bf16[1,1,4,4,64,128]{5,4,3,2,1,0:T(8,128)(2,1)} %collective-permute-done.2, ...), kind=kOutput, calls=%fused_computation.227 | convolution fusion | flops 39583744 | bytes 7344128 | tf_op jit(solution)/shard_map/tzxyab,tzxybr->tzxyar/dot_general | solution.py:18
  68.2 1.9 %collective-permute-start.5 = (bf16[1,2,4,4,64,128]{5,4,3,2,1,0:T(8,128)(2,1)S(1)}, bf16[1,2,4,4,64,128]{5,4,3,2,1,0:T(8,128)(2,1)S(1)}, u32[]{:S(2)}, u32[]{:S(2)}) collective-permute-start(bf16[1,2,4,4,64,128]{5,4,3,2,1,0:T(8,128)(2,1)S(1)} %get-tuple-element.19), channel_id=1, source_target_pairs={{4,0},{8,4},{12,8},{16,12},{20,16},{24,20},{28,24},{32,28},{36,32}... | collective-permute-start | bytes 1572872 | tf_op jit(solution)/shard_map/ppermute | solution.py:14
  70.2 0.4 fusion.62
  70.5 0.6 fusion.61
  71.2 0.4 fusion.64
  71.7 2.1 %collective-permute-start.6 = (bf16[1,1,4,4,64,128]{5,4,3,2,1,0:T(8,128)(2,1)S(1)}, bf16[1,1,4,4,64,128]{5,4,3,2,1,0:T(8,128)(2,1)S(1)}, u32[]{:S(2)}, u32[]{:S(2)}) collective-permute-start(bf16[1,1,4,4,64,128]{5,4,3,2,1,0:T(8,128)(2,1)S(1)} %get-tuple-element.11), channel_id=1, source_target_pairs={{3,0},{0,1},{1,2},{2,3},{7,4},{4,5},{5,6},{6,7},{11,8},{8,9},{9,10... | collective-permute-start | bytes 786440 | tf_op jit(solution)/shard_map/ppermute | solution.py:14
  73.8 3.6 %collective-permute-start.7 = (bf16[1,2,4,4,64,128]{5,4,3,2,1,0:T(8,128)(2,1)S(1)}, bf16[1,2,4,4,64,128]{5,4,3,2,1,0:T(8,128)(2,1)S(1)}, u32[]{:S(2)}, u32[]{:S(2)}) collective-permute-start(bf16[1,2,4,4,64,128]{5,4,3,2,1,0:T(8,128)(2,1)S(1)} %fusion.61), channel_id=1, source_target_pairs={{508,0},{0,4},{4,8},{8,12},{12,16},{16,20},{20,24},{24,28},{28,32}... | collective-permute-start | bytes 1572872 | tf_op jit(solution)/shard_map/ppermute | solution.py:14
  77.4 2.8 %collective-permute-start.4 = (bf16[1,1,4,4,64,128]{5,4,3,2,1,0:T(8,128)(2,1)S(1)}, bf16[1,1,4,4,64,128]{5,4,3,2,1,0:T(8,128)(2,1)S(1)}, u32[]{:S(2)}, u32[]{:S(2)}) collective-permute-start(bf16[1,1,4,4,64,128]{5,4,3,2,1,0:T(8,128)(2,1)S(1)} %get-tuple-element.14), channel_id=1, source_target_pairs={{1,0},{2,1},{3,2},{0,3},{5,4},{6,5},{7,6},{4,7},{9,8},{10,9},{11,1... | collective-permute-start | bytes 786440 | tf_op jit(solution)/shard_map/ppermute | solution.py:14
  81.3 0.6 fusion.63
  82.0 10.6 %collective-permute-done.5 = bf16[1,2,4,4,64,128]{5,4,3,2,1,0:T(8,128)(2,1)S(1)} collective-permute-done((bf16[1,2,4,4,64,128]{5,4,3,2,1,0:T(8,128)(2,1)S(1)}, bf16[1,2,4,4,64,128]{5,4,3,2,1,0:T(8,128)(2,1)S(1)}, u32[]{:S(2)}, u32[]{:S(2)}) %collective-permute-start.5) | collective-permute-done | bytes 524320 | tf_op jit(solution)/shard_map/ppermute | solution.py:14
  93.0 10.2 %collective-permute-done.7 = bf16[1,2,4,4,64,128]{5,4,3,2,1,0:T(8,128)(2,1)S(1)} collective-permute-done((bf16[1,2,4,4,64,128]{5,4,3,2,1,0:T(8,128)(2,1)S(1)}, bf16[1,2,4,4,64,128]{5,4,3,2,1,0:T(8,128)(2,1)S(1)}, u32[]{:S(2)}, u32[]{:S(2)}) %collective-permute-start.7) | collective-permute-done | bytes 524320 | tf_op jit(solution)/shard_map/ppermute | solution.py:14
  103.2 0.7 fusion.179
  104.0 1.9 %collective-permute-start.9 = (bf16[1,2,4,4,64,128]{5,4,3,2,1,0:T(8,128)(2,1)S(1)}, bf16[1,2,4,4,64,128]{5,4,3,2,1,0:T(8,128)(2,1)S(1)}, u32[]{:S(2)}, u32[]{:S(2)}) collective-permute-start(bf16[1,2,4,4,64,128]{5,4,3,2,1,0:T(8,128)(2,1)S(1)} %get-tuple-element.21), channel_id=1, source_target_pairs={{4,0},{8,4},{12,8},{16,12},{20,16},{24,20},{28,24},{32,28},{36,32}... | collective-permute-start | bytes 1572872 | tf_op jit(solution)/shard_map/ppermute | solution.py:14
  105.9 0.4 fusion.58
  106.3 0.6 fusion.57
  106.9 0.4 fusion.60
  107.4 7.5 %collective-permute-start.10 = (bf16[1,1,4,4,64,128]{5,4,3,2,1,0:T(8,128)(2,1)S(1)}, bf16[1,1,4,4,64,128]{5,4,3,2,1,0:T(8,128)(2,1)S(1)}, u32[]{:S(2)}, u32[]{:S(2)}) collective-permute-start(bf16[1,1,4,4,64,128]{5,4,3,2,1,0:T(8,128)(2,1)S(1)} %get-tuple-element.7), channel_id=1, source_target_pairs={{3,0},{0,1},{1,2},{2,3},{7,4},{4,5},{5,6},{6,7},{11,8},{8,9},{9,10... | collective-permute-start | bytes 786440 | tf_op jit(solution)/shard_map/ppermute | solution.py:14
  114.9 3.6 %collective-permute-start.11 = (bf16[1,2,4,4,64,128]{5,4,3,2,1,0:T(8,128)(2,1)S(1)}, bf16[1,2,4,4,64,128]{5,4,3,2,1,0:T(8,128)(2,1)S(1)}, u32[]{:S(2)}, u32[]{:S(2)}) collective-permute-start(bf16[1,2,4,4,64,128]{5,4,3,2,1,0:T(8,128)(2,1)S(1)} %fusion.57), channel_id=1, source_target_pairs={{508,0},{0,4},{4,8},{8,12},{12,16},{16,20},{20,24},{24,28},{28,32}... | collective-permute-start | bytes 1572872 | tf_op jit(solution)/shard_map/ppermute | solution.py:14
  118.5 2.1 %collective-permute-start.8 = (bf16[1,1,4,4,64,128]{5,4,3,2,1,0:T(8,128)(2,1)S(1)}, bf16[1,1,4,4,64,128]{5,4,3,2,1,0:T(8,128)(2,1)S(1)}, u32[]{:S(2)}, u32[]{:S(2)}) collective-permute-start(bf16[1,1,4,4,64,128]{5,4,3,2,1,0:T(8,128)(2,1)S(1)} %get-tuple-element.10), channel_id=1, source_target_pairs={{1,0},{2,1},{3,2},{0,3},{5,4},{6,5},{7,6},{4,7},{9,8},{10,9},{11,1... | collective-permute-start | bytes 786440 | tf_op jit(solution)/shard_map/ppermute | solution.py:14
  121.4 0.4 fusion.35
  121.8 0.6 fusion.59
  122.8 13.7 %collective-permute-done.8 = bf16[1,1,4,4,64,128]{5,4,3,2,1,0:T(8,128)(2,1)S(1)} collective-permute-done((bf16[1,1,4,4,64,128]{5,4,3,2,1,0:T(8,128)(2,1)S(1)}, bf16[1,1,4,4,64,128]{5,4,3,2,1,0:T(8,128)(2,1)S(1)}, u32[]{:S(2)}, u32[]{:S(2)}) %collective-permute-start.8) | collective-permute-done | bytes 262176 | tf_op jit(solution)/shard_map/ppermute | solution.py:14
  136.5 10.0 %collective-permute-done.11 = bf16[1,2,4,4,64,128]{5,4,3,2,1,0:T(8,128)(2,1)S(1)} collective-permute-done((bf16[1,2,4,4,64,128]{5,4,3,2,1,0:T(8,128)(2,1)S(1)}, bf16[1,2,4,4,64,128]{5,4,3,2,1,0:T(8,128)(2,1)S(1)}, u32[]{:S(2)}, u32[]{:S(2)}) %collective-permute-start.11) | collective-permute-done | bytes 524320 | tf_op jit(solution)/shard_map/ppermute | solution.py:14
  146.6 0.7 fusion.44
  147.9 0.4 copy-done.13
  148.3 1.9 %fusion.69 = f32[16,8192]{1,0:T(8,128)} fusion(f32[4,8,64,128]{3,2,1,0:T(8,128)S(1)} %bitcast.321, s32[32]{0:T(128)S(1)} %copy-done.13), kind=kOutput, calls=%fused_computation.101 | convolution fusion | flops 50332160 | bytes 1572992 | tf_op jit(solution)/shard_map/dot_general | solution.py:75
  150.2 27.6 %all-gather.3.cloned.1.call-done = f32[64,8192]{1,0:T(8,128)} async-done(((f32[16,8192]{1,0:T(8,128)}), f32[64,8192]{1,0:T(8,128)}) %all-gather.3.cloned.1.call-update) | async-done | bytes 2097168 | tf_op jit(solution)/shard_map/all_gather | solution.py:76
  177.8 1.8 reduce_sum.9
  179.6 0.7 copy.51
  (80 shorter events, 4.4 us)
Async XLA Ops:
  7.2 30.3 %copy-start = (bf16[1,2,4,4,64,64]{5,4,3,2,1,0:T(8,128)(2,1)S(1)}, bf16[1,2,4,4,64,64]{5,4,3,2,1,0:T(8,128)(2,1)}, u32[]{:S(2)}) copy-start(bf16[1,2,4,4,64,64]{5,4,3,2,1,0:T(8,128)(2,1)} %param.7) | copy-start | bytes 786436
  7.2 24.1 %copy-start.2 = (bf16[1,2,4,4,64,128]{5,4,3,2,1,0:T(8,128)(2,1)S(1)}, bf16[1,2,4,4,64,128]{5,4,3,2,1,0:T(8,128)(2,1)}, u32[]{:S(2)}) copy-start(bf16[1,2,4,4,64,128]{5,4,3,2,1,0:T(8,128)(2,1)} %param.6) | copy-start | bytes 1572868
  7.2 24.1 %copy-start.1 = (bf16[1,2,4,4,64,256]{5,4,3,2,1,0:T(8,128)(2,1)S(1)}, bf16[1,2,4,4,64,256]{5,4,3,2,1,0:T(8,128)(2,1)}, u32[]{:S(2)}) copy-start(bf16[1,2,4,4,64,256]{5,4,3,2,1,0:T(8,128)(2,1)} %param.8) | copy-start | bytes 3145732
  7.2 170.6 %all-gather.3.cloned.1.call-start = ((), (), s32[]{:S(2)}) async-start(), calls=%async_computation | async-start | bytes 2621440 | tf_op jit(solution)/shard_map/all_gather | solution.py:76
  7.2 39.7 %collective-permute-start.1 = (bf16[1,2,4,4,64,128]{5,4,3,2,1,0:T(8,128)(2,1)}, bf16[1,2,4,4,64,128]{5,4,3,2,1,0:T(8,128)(2,1)}, u32[]{:S(2)}, u32[]{:S(2)}) collective-permute-start(bf16[1,2,4,4,64,128]{5,4,3,2,1,0:T(8,128)(2,1)} %param.6), channel_id=1, source_target_pairs={{4,0},{8,4},{12,8},{16,12},{20,16},{24,20},{28,24},{32,28},{36,32}... | collective-permute-start | bytes 1572872 | tf_op jit(solution)/shard_map/ppermute | solution.py:14
  25.7 11.8 %copy-start.11 = (f32[2,4,4]{2,1,0:T(4,128)}, f32[2,4,4]{2,1,0:T(4,128)S(1)}, u32[]{:S(2)}) copy-start(f32[2,4,4]{2,1,0:T(4,128)S(1)} %get-tuple-element.6) | copy-start | bytes 388
  28.1 20.2 %collective-permute-start.2 = (bf16[1,1,4,4,64,128]{5,4,3,2,1,0:T(8,128)(2,1)}, bf16[1,1,4,4,64,128]{5,4,3,2,1,0:T(8,128)(2,1)}, u32[]{:S(2)}, u32[]{:S(2)}) collective-permute-start(bf16[1,1,4,4,64,128]{5,4,3,2,1,0:T(8,128)(2,1)} %get-tuple-element.15), channel_id=1, source_target_pairs={{3,0},{0,1},{1,2},{2,3},{7,4},{4,5},{5,6},{6,7},{11,8},{8,9},{9,10... | collective-permute-start | bytes 786440 | tf_op jit(solution)/shard_map/ppermute | solution.py:14
  32.7 33.5 %collective-permute-start.3 = (bf16[1,2,4,4,64,128]{5,4,3,2,1,0:T(8,128)(2,1)}, bf16[1,2,4,4,64,128]{5,4,3,2,1,0:T(8,128)(2,1)}, u32[]{:S(2)}, u32[]{:S(2)}) collective-permute-start(bf16[1,2,4,4,64,128]{5,4,3,2,1,0:T(8,128)(2,1)} %fusion.65), channel_id=1, source_target_pairs={{508,0},{0,4},{4,8},{8,12},{12,16},{16,20},{20,24},{24,28},{28,32}... | collective-permute-start | bytes 1572872 | tf_op jit(solution)/shard_map/ppermute | solution.py:14
  35.5 18.3 %collective-permute-start = (bf16[1,1,4,4,64,128]{5,4,3,2,1,0:T(8,128)(2,1)}, bf16[1,1,4,4,64,128]{5,4,3,2,1,0:T(8,128)(2,1)}, u32[]{:S(2)}, u32[]{:S(2)}) collective-permute-start(bf16[1,1,4,4,64,128]{5,4,3,2,1,0:T(8,128)(2,1)} %get-tuple-element.18), channel_id=1, source_target_pairs={{1,0},{2,1},{3,2},{0,3},{5,4},{6,5},{7,6},{4,7},{9,8},{10,9},{11,1... | collective-permute-start | bytes 786440 | tf_op jit(solution)/shard_map/ppermute | solution.py:14
  38.5 0.8 copy-start.4
  39.6 26.6 %slice-start.2 = ((bf16[1,2,4,4,64,128]{5,4,3,2,1,0:T(8,128)(2,1)}), bf16[1,2,3,4,64,128]{5,4,3,2,1,0:T(8,128)(2,1)S(1)}, s32[]{:S(2)}) async-start(bf16[1,2,4,4,64,128]{5,4,3,2,1,0:T(8,128)(2,1)} %copy-done.4), calls=%async_computation.3 | async-start | bytes 786432 | tf_op jit(solution)/shard_map/jit(_roll_static)/slice | solution.py:53
  40.2 0.8 copy-start.5
  42.4 23.9 %slice-start.3 = ((bf16[1,2,4,4,64,128]{5,4,3,2,1,0:T(8,128)(2,1)}), bf16[1,2,1,4,64,128]{5,4,3,2,1,0:T(8,128)(2,1)S(1)}, s32[]{:S(2)}) async-start(bf16[1,2,4,4,64,128]{5,4,3,2,1,0:T(8,128)(2,1)} %copy-done.4), calls=%async_computation.4 | async-start | bytes 262144 | tf_op jit(solution)/shard_map/jit(_roll_static)/slice | solution.py:53
  42.4 23.9 %slice-start.4 = ((bf16[1,2,4,4,64,128]{5,4,3,2,1,0:T(8,128)(2,1)}), bf16[1,2,4,3,64,128]{5,4,3,2,1,0:T(8,128)(2,1)S(1)}, s32[]{:S(2)}) async-start(bf16[1,2,4,4,64,128]{5,4,3,2,1,0:T(8,128)(2,1)} %copy-done.5), calls=%async_computation.5 | async-start | bytes 786432 | tf_op jit(solution)/shard_map/jit(_roll_static)/slice | solution.py:53
  42.4 23.9 %slice-start.5 = ((bf16[1,2,4,4,64,128]{5,4,3,2,1,0:T(8,128)(2,1)}), bf16[1,2,4,1,64,128]{5,4,3,2,1,0:T(8,128)(2,1)S(1)}, s32[]{:S(2)}) async-start(bf16[1,2,4,4,64,128]{5,4,3,2,1,0:T(8,128)(2,1)} %copy-done.5), calls=%async_computation.6 | async-start | bytes 262144 | tf_op jit(solution)/shard_map/jit(_roll_static)/slice | solution.py:53
  42.4 23.9 %copy-start.8 = (bf16[1,1,4,4,64,128]{5,4,3,2,1,0:T(8,128)(2,1)S(1)}, bf16[1,1,4,4,64,128]{5,4,3,2,1,0:T(8,128)(2,1)}, u32[]{:S(2)}) copy-start(bf16[1,1,4,4,64,128]{5,4,3,2,1,0:T(8,128)(2,1)} %get-tuple-element.16) | copy-start | bytes 786436
  42.4 23.9 %copy-start.9 = (bf16[1,1,4,4,64,128]{5,4,3,2,1,0:T(8,128)(2,1)S(1)}, bf16[1,1,4,4,64,128]{5,4,3,2,1,0:T(8,128)(2,1)}, u32[]{:S(2)}) copy-start(bf16[1,1,4,4,64,128]{5,4,3,2,1,0:T(8,128)(2,1)} %get-tuple-element.17) | copy-start | bytes 786436
  68.2 24.3 %collective-permute-start.5 = (bf16[1,2,4,4,64,128]{5,4,3,2,1,0:T(8,128)(2,1)S(1)}, bf16[1,2,4,4,64,128]{5,4,3,2,1,0:T(8,128)(2,1)S(1)}, u32[]{:S(2)}, u32[]{:S(2)}) collective-permute-start(bf16[1,2,4,4,64,128]{5,4,3,2,1,0:T(8,128)(2,1)S(1)} %get-tuple-element.19), channel_id=1, source_target_pairs={{4,0},{8,4},{12,8},{16,12},{20,16},{24,20},{28,24},{32,28},{36,32}... | collective-permute-start | bytes 1572872 | tf_op jit(solution)/shard_map/ppermute | solution.py:14
  71.5 9.0 %copy-start.6 = (bf16[1,2,4,4,64,128]{5,4,3,2,1,0:T(8,128)(2,1)}, bf16[1,2,4,4,64,128]{5,4,3,2,1,0:T(8,128)(2,1)S(1)}, u32[]{:S(2)}) copy-start(bf16[1,2,4,4,64,128]{5,4,3,2,1,0:T(8,128)(2,1)S(1)} %fusion.64) | copy-start | bytes 1572868
  71.6 9.0 %copy-start.12 = (f32[2,4,4]{2,1,0:T(4,128)S(1)}, f32[2,4,4]{2,1,0:T(4,128)}, u32[]{:S(2)}) copy-start(f32[2,4,4]{2,1,0:T(4,128)} %copy-done.11) | copy-start | bytes 388
  71.7 21.3 %collective-permute-start.6 = (bf16[1,1,4,4,64,128]{5,4,3,2,1,0:T(8,128)(2,1)S(1)}, bf16[1,1,4,4,64,128]{5,4,3,2,1,0:T(8,128)(2,1)S(1)}, u32[]{:S(2)}, u32[]{:S(2)}) collective-permute-start(bf16[1,1,4,4,64,128]{5,4,3,2,1,0:T(8,128)(2,1)S(1)} %get-tuple-element.11), channel_id=1, source_target_pairs={{3,0},{0,1},{1,2},{2,3},{7,4},{4,5},{5,6},{6,7},{11,8},{8,9},{9,10... | collective-permute-start | bytes 786440 | tf_op jit(solution)/shard_map/ppermute | solution.py:14
  73.8 29.4 %collective-permute-start.7 = (bf16[1,2,4,4,64,128]{5,4,3,2,1,0:T(8,128)(2,1)S(1)}, bf16[1,2,4,4,64,128]{5,4,3,2,1,0:T(8,128)(2,1)S(1)}, u32[]{:S(2)}, u32[]{:S(2)}) collective-permute-start(bf16[1,2,4,4,64,128]{5,4,3,2,1,0:T(8,128)(2,1)S(1)} %fusion.61), channel_id=1, source_target_pairs={{508,0},{0,4},{4,8},{8,12},{12,16},{16,20},{20,24},{24,28},{28,32}... | collective-permute-start | bytes 1572872 | tf_op jit(solution)/shard_map/ppermute | solution.py:14
  77.4 15.5 %collective-permute-start.4 = (bf16[1,1,4,4,64,128]{5,4,3,2,1,0:T(8,128)(2,1)S(1)}, bf16[1,1,4,4,64,128]{5,4,3,2,1,0:T(8,128)(2,1)S(1)}, u32[]{:S(2)}, u32[]{:S(2)}) collective-permute-start(bf16[1,1,4,4,64,128]{5,4,3,2,1,0:T(8,128)(2,1)S(1)} %get-tuple-element.14), channel_id=1, source_target_pairs={{1,0},{2,1},{3,2},{0,3},{5,4},{6,5},{7,6},{4,7},{9,8},{10,9},{11,1... | collective-permute-start | bytes 786440 | tf_op jit(solution)/shard_map/ppermute | solution.py:14
  81.3 21.9 %slice-start.6 = ((bf16[1,2,4,4,64,128]{5,4,3,2,1,0:T(8,128)(2,1)}), bf16[1,2,3,4,64,128]{5,4,3,2,1,0:T(8,128)(2,1)S(1)}, s32[]{:S(2)}) async-start(bf16[1,2,4,4,64,128]{5,4,3,2,1,0:T(8,128)(2,1)} %copy-done.6), calls=%async_computation.7 | async-start | bytes 786432 | tf_op jit(solution)/shard_map/jit(_roll_static)/slice | solution.py:53
  81.3 21.9 %slice-start.7 = ((bf16[1,2,4,4,64,128]{5,4,3,2,1,0:T(8,128)(2,1)}), bf16[1,2,1,4,64,128]{5,4,3,2,1,0:T(8,128)(2,1)S(1)}, s32[]{:S(2)}) async-start(bf16[1,2,4,4,64,128]{5,4,3,2,1,0:T(8,128)(2,1)} %copy-done.6), calls=%async_computation.8 | async-start | bytes 262144 | tf_op jit(solution)/shard_map/jit(_roll_static)/slice | solution.py:53
  104.0 18.5 %collective-permute-start.9 = (bf16[1,2,4,4,64,128]{5,4,3,2,1,0:T(8,128)(2,1)S(1)}, bf16[1,2,4,4,64,128]{5,4,3,2,1,0:T(8,128)(2,1)S(1)}, u32[]{:S(2)}, u32[]{:S(2)}) collective-permute-start(bf16[1,2,4,4,64,128]{5,4,3,2,1,0:T(8,128)(2,1)S(1)} %get-tuple-element.21), channel_id=1, source_target_pairs={{4,0},{8,4},{12,8},{16,12},{20,16},{24,20},{28,24},{32,28},{36,32}... | collective-permute-start | bytes 1572872 | tf_op jit(solution)/shard_map/ppermute | solution.py:14
  107.3 13.7 %copy-start.3 = (bf16[1,2,4,4,64,128]{5,4,3,2,1,0:T(8,128)(2,1)}, bf16[1,2,4,4,64,128]{5,4,3,2,1,0:T(8,128)(2,1)S(1)}, u32[]{:S(2)}) copy-start(bf16[1,2,4,4,64,128]{5,4,3,2,1,0:T(8,128)(2,1)S(1)} %fusion.60) | copy-start | bytes 1572868
  107.4 15.5 %collective-permute-start.10 = (bf16[1,1,4,4,64,128]{5,4,3,2,1,0:T(8,128)(2,1)S(1)}, bf16[1,1,4,4,64,128]{5,4,3,2,1,0:T(8,128)(2,1)S(1)}, u32[]{:S(2)}, u32[]{:S(2)}) collective-permute-start(bf16[1,1,4,4,64,128]{5,4,3,2,1,0:T(8,128)(2,1)S(1)} %get-tuple-element.7), channel_id=1, source_target_pairs={{3,0},{0,1},{1,2},{2,3},{7,4},{4,5},{5,6},{6,7},{11,8},{8,9},{9,10... | collective-permute-start | bytes 786440 | tf_op jit(solution)/shard_map/ppermute | solution.py:14
  114.9 31.7 %collective-permute-start.11 = (bf16[1,2,4,4,64,128]{5,4,3,2,1,0:T(8,128)(2,1)S(1)}, bf16[1,2,4,4,64,128]{5,4,3,2,1,0:T(8,128)(2,1)S(1)}, u32[]{:S(2)}, u32[]{:S(2)}) collective-permute-start(bf16[1,2,4,4,64,128]{5,4,3,2,1,0:T(8,128)(2,1)S(1)} %fusion.57), channel_id=1, source_target_pairs={{508,0},{0,4},{4,8},{8,12},{12,16},{16,20},{20,24},{24,28},{28,32}... | collective-permute-start | bytes 1572872 | tf_op jit(solution)/shard_map/ppermute | solution.py:14
  118.5 18.0 %collective-permute-start.8 = (bf16[1,1,4,4,64,128]{5,4,3,2,1,0:T(8,128)(2,1)S(1)}, bf16[1,1,4,4,64,128]{5,4,3,2,1,0:T(8,128)(2,1)S(1)}, u32[]{:S(2)}, u32[]{:S(2)}) collective-permute-start(bf16[1,1,4,4,64,128]{5,4,3,2,1,0:T(8,128)(2,1)S(1)} %get-tuple-element.10), channel_id=1, source_target_pairs={{1,0},{2,1},{3,2},{0,3},{5,4},{6,5},{7,6},{4,7},{9,8},{10,9},{11,1... | collective-permute-start | bytes 786440 | tf_op jit(solution)/shard_map/ppermute | solution.py:14
  121.7 24.8 %slice-start = ((bf16[1,2,4,4,64,128]{5,4,3,2,1,0:T(8,128)(2,1)}), bf16[1,2,3,4,64,128]{5,4,3,2,1,0:T(8,128)(2,1)S(1)}, s32[]{:S(2)}) async-start(bf16[1,2,4,4,64,128]{5,4,3,2,1,0:T(8,128)(2,1)} %copy-done.3), calls=%async_computation.1 | async-start | bytes 786432 | tf_op jit(solution)/shard_map/jit(_roll_static)/slice | solution.py:53
  121.8 24.8 %slice-start.1 = ((bf16[1,2,4,4,64,128]{5,4,3,2,1,0:T(8,128)(2,1)}), bf16[1,2,1,4,64,128]{5,4,3,2,1,0:T(8,128)(2,1)S(1)}, s32[]{:S(2)}) async-start(bf16[1,2,4,4,64,128]{5,4,3,2,1,0:T(8,128)(2,1)} %copy-done.3), calls=%async_computation.2 | async-start | bytes 262144 | tf_op jit(solution)/shard_map/jit(_roll_static)/slice | solution.py:53
  146.6 1.0 copy-start.10
  147.6 2.6 %copy-start.7 = (bf16[1,2,4,4,64,128]{5,4,3,2,1,0:T(8,128)(2,1)}, bf16[1,2,4,4,64,128]{5,4,3,2,1,0:T(8,128)(2,1)S(1)}, u32[]{:S(2)}) copy-start(bf16[1,2,4,4,64,128]{5,4,3,2,1,0:T(8,128)(2,1)S(1)} %fusion.44) | copy-start | bytes 1572868
  147.6 0.7 copy-start.13
Sparse Core Ops, SparseCore 0:
  150.3 27.4 all-gather.2
